TPU v7x, 128 devices: a whole 4x4x4 slice. The times are simulated.
128 devices in a mesh: dp: 128 (over z, y, x, core).
Axes of the slice: x: 4, y: 4, z: 4, core: 2. Of those that a mesh axis runs over, the one named last changes fastest.
Arguments:
- embeddings: bfloat16 [131072, 1024], P('dp')
- partners: int32 [128, 13], P('dp'), may hold values from 0 to 127, as said below
- pair_count: int32 [128], P('dp'), may hold values from 1 to 13, as said below
Outputs:
- soft_cosine: float32 [131072], P('dp')
Inputs may be any that keep to these rules, and one draw needn't show every extreme that they name: Entry 0 of partners[h] is h; the live entries of partners[h] are distinct blocks from h to min(h + 16, 127), so each unordered pair of blocks stands once; entries past pair_count[h] are arbitrary blocks in that range and are not pairs. `pair_count`: at most 13 live pairs for one block; some block has exactly 13.
All inputs are finite; a program needn't handle non-finite values.
Results may differ from a plain program's by a relative error of at most 0.00043.
Values may be sent and summed in bfloat16 or wider, within the bound.
No kernel may reach another device: no remote copies, remote signals or barrier semaphores. Data moves between devices by JAX's collectives and lax.ppermute only.
A program may use at most 128 MiB of HBM per device.

v0:
```python
import functools

import jax
import jax.numpy as jnp
from jax import lax
from jax.experimental import pallas as pl
from jax.experimental.pallas import tpu as pltpu
from jax.sharding import PartitionSpec as P

SCALE = 256.0
LOG2E = 1.4426950408889634
LN2 = 0.6931471805599453
GAIN = SCALE * LOG2E
PLAIN = 78.0 / SCALE
FLOOR = -1e30
MASKED = -1e27
SCRATCH = 17
PLACES = [(0, 0), (0, 1), (3, 0), (1, 0), (3, 1), (1, 1), (2, 0), (2, 1)]
B = 1024
D = 1024
H = B // 2
CH = 256
G = 32
COUNT = 128
RING = 8
HALVES = B // 2 // CH
LIST = 16
GRANT = 62 * 2**20


def around(dx):
    moves = []
    for d in range(COUNT):
        core, x, rest = d % 2, (d // 2) % 4, d // RING
        moves.append((d, rest * RING + ((x + dx) % 4) * 2 + core))
    return moves


def along(steps, flip=0):
    return [(d, (d + steps) ^ flip) for d in range(COUNT) if 0 <= d + steps < COUNT]


def send(value, moves):
    return lax.ppermute(value, "dp", moves)


def unit_kernel(list_ref, count_ref, x_ref, o_ref, top_ref, low_ref, x, o, in_sem, out_sem):
    def rows(i):
        return pl.ds(i * CH, CH)

    loads = [pltpu.make_async_copy(x_ref.at[rows(i), :], x.at[rows(i), :], in_sem.at[i]) for i in range(B // CH)]
    for load in loads:
        load.start()
    lane = lax.broadcasted_iota(jnp.int32, (LIST, D), 1)
    pairs = jnp.full((LIST, D), -1.0, jnp.float32)
    for k in range(list_ref.shape[1]):
        entry = jnp.where(k < count_ref[0], list_ref[0, k], -1).astype(jnp.float32)
        pairs = jnp.where(lane == k, entry, pairs)
    o[B : B + LIST, :] = pairs.astype(jnp.bfloat16)
    stores = [pltpu.make_async_copy(o.at[pl.ds(B, LIST), :], o_ref.at[pl.ds(B, LIST), :], out_sem.at[0])]
    stores[0].start()
    for i in range(B // CH):
        loads[i].wait()
        for g in range(CH // G):
            at = slice(i * CH + g * G, i * CH + (g + 1) * G)
            v = x[at, :].astype(jnp.float32)
            size = jnp.sum(v * v, -1, keepdims=True)
            o[at, :] = (v * lax.rsqrt(size + 1e-06)).astype(jnp.bfloat16)
        stores.append(pltpu.make_async_copy(o.at[rows(i), :], o_ref.at[rows(i), :], out_sem.at[2 * i + 1]))
        half = top_ref.at[rows(i), :] if i < HALVES else low_ref.at[rows(i - HALVES), :]
        stores.append(pltpu.make_async_copy(o.at[rows(i), :], half, out_sem.at[2 * i + 2]))
        stores[-2].start()
        stores[-1].start()
    for store in stores:
        store.wait()


def normalize(embeddings, partners, pair_count):
    bf16 = jnp.bfloat16
    smem, anywhere = pl.BlockSpec(memory_space=pltpu.SMEM), pl.BlockSpec(memory_space=pl.ANY)
    return pl.pallas_call(
        unit_kernel,
        in_specs=[smem, smem, anywhere],
        out_specs=[anywhere] * 3,
        out_shape=[
            jax.ShapeDtypeStruct((B + LIST, D), bf16),
            jax.ShapeDtypeStruct((B // 2, D), bf16),
            jax.ShapeDtypeStruct((B // 2, D), bf16),
        ],
        scratch_shapes=[
            pltpu.VMEM((B, D), bf16),
            pltpu.VMEM((B + LIST, D), bf16),
            pltpu.SemaphoreType.DMA((B // CH,)),
            pltpu.SemaphoreType.DMA((2 * (B // CH) + 1,)),
        ],
        compiler_params=pltpu.CompilerParams(vmem_limit_bytes=GRANT),
        name="unit_rows",
    )(partners, pair_count, embeddings)


def halves_kernel(a_ref, b_ref, top_ref, low_ref, buf, sem):
    n = B // 2 // CH
    moves = []
    for i in range(2 * n):
        count = CH + LIST if i == 2 * n - 1 else CH
        src = a_ref.at[pl.ds(i * CH, count), :] if i < n else b_ref.at[pl.ds(i * CH, count), :]
        dst = top_ref.at[pl.ds(i * CH, count), :] if i < n else low_ref.at[pl.ds((i - n) * CH, count), :]
        held = buf.at[pl.ds(i * CH, count), :]
        moves.append((pltpu.make_async_copy(src, held, sem.at[2 * i]), pltpu.make_async_copy(held, dst, sem.at[2 * i + 1])))
    for load, _ in moves:
        load.start()
    for load, store in moves:
        load.wait()
        store.start()
    for _, store in moves:
        store.wait()


def halves(a, b):
    bf16, anywhere = jnp.bfloat16, pl.BlockSpec(memory_space=pl.ANY)
    return pl.pallas_call(
        halves_kernel,
        in_specs=[anywhere] * 2,
        out_specs=[anywhere] * 2,
        out_shape=[jax.ShapeDtypeStruct((B // 2, D), bf16), jax.ShapeDtypeStruct((B // 2 + LIST, D), bf16)],
        scratch_shapes=[pltpu.VMEM((B + LIST, D), bf16), pltpu.SemaphoreType.DMA((2 * B // CH,))],
        compiler_params=pltpu.CompilerParams(vmem_limit_bytes=GRANT),
        name="halves",
    )(a, b)


def lanes(value, op):
    return functools.reduce(op, [value[:, q * 128 : (q + 1) * 128] for q in range(value.shape[1] // 128)])


def rows8(value, op):
    return functools.reduce(op, [value[q * 8 : (q + 1) * 8, :] for q in range(value.shape[0] // 8)])


def fold(m, s, f, axis):
    top = jnp.max(m, axis, keepdims=True)
    plain = jnp.sum(f, axis, keepdims=True)
    top = jnp.maximum(top, jnp.where(plain > 0.0, 0.0, FLOOR))
    total = jnp.sum(s * jnp.exp2(m - top), axis, keepdims=True)
    total = total + plain * jnp.exp2(jnp.minimum(-top, 0.0))
    return jnp.maximum(top + jnp.log2(total), FLOOR)


def log2_add(a, b):
    top = jnp.maximum(a, b)
    return top + jnp.log2(jnp.exp2(a - top) + jnp.exp2(b - top))


def stage_kernel(plan, live, *refs):
    nl, nr, lefts, rights, widths, nrow, ncol, own_first, last = plan
    row_prev, col_prev, refs = refs[: len(nrow)], refs[len(nrow) : len(nrow) + len(ncol)], refs[len(nrow) + len(ncol) :]
    blocks, refs = refs[: len(lefts) + len(rights)], refs[len(lefts) + len(rights) :]
    outs, refs = refs[:-SCRATCH], refs[-SCRATCH:]
    row_out, col_out = refs[-2:] if last else outs
    (lbuf, rbuf, sc, row_t, col_t, chk, row_f, row_m, row_s, col_f, col_m, col_s, waited, lsem, rsem) = refs[:-2]

    def copies(side, slot):
        pieces = lefts if side == 0 else rights
        base = 0 if side == 0 else len(lefts)
        buf, sem = (lbuf, lsem) if side == 0 else (rbuf, rsem)
        made = []
        for i, (s, src, dst, count) in enumerate(pieces):
            if s == slot:
                made.append(
                    pltpu.make_async_copy(
                        blocks[base + i].at[pl.ds(src, count), :], buf.at[slot, pl.ds(dst, count), :], sem.at[slot]
                    )
                )
        return made

    def used(flags):
        return functools.reduce(jnp.logical_or, [f > 0 for f in flags])

    need_l = [used([live[q * nr + r] for r in range(nr)]) for q in range(nl)]
    need_r = [used([live[q * nr + r] for q in range(nl)]) for r in range(nr)]
    for r in range(nr):
        waited[r] = 0

        @pl.when(need_r[r])
        def _(r=r):
            for c in copies(1, r):
                c.start()

    for q in range(nl):

        @pl.when(need_l[q])
        def _(q=q):
            for c in copies(0, q):
                c.start()

    col_f[...] = jnp.zeros_like(col_f)
    col_s[...] = jnp.zeros_like(col_s)
    col_m[...] = jnp.full_like(col_m, FLOOR)

    def pair(q, r, width, diag):
        def dot(i):
            sc[i * CH : (i + 1) * CH, :width] = lax.dot_general(
                lbuf[q, i * CH : (i + 1) * CH, :],
                rbuf[r, :width, :],
                (((1,), (1,)), ((), ())),
                preferred_element_type=jnp.float32,
            )

        def sums(i):
            cols = jnp.zeros((8, width), jnp.float32)
            size = jnp.zeros((8, 128), jnp.float32)
            for g in range(CH // G):
                at = i * CH + g * G
                v = sc[at : at + G, :width]
                if diag:
                    r_at = lax.broadcasted_iota(jnp.int32, (G, width), 0) + at
                    c_at = lax.broadcasted_iota(jnp.int32, (G, width), 1)
                    eye = r_at == c_at
                    absv = jnp.where(eye, 0.0, jnp.abs(v))
                    v = jnp.where(eye, MASKED, v)
                    sc[at : at + G, :width] = v
                else:
                    absv = jnp.abs(v)
                e = jnp.exp2(v * GAIN)
                row_t[at : at + G, :] = lanes(e, jnp.add)
                if not diag:
                    cols = cols + rows8(e, jnp.add)
                size = jnp.maximum(size, rows8(lanes(absv, jnp.maximum), jnp.maximum))
            if not diag:
                col_t[:, :width] = cols if i == 0 else col_t[:, :width] + cols
            chk[...] = size if i == 0 else jnp.maximum(chk[...], size)

        n = B // CH
        dot(0)
        for i in range(n):
            if i + 1 < n:
                dot(i + 1)
            sums(i)
        plain = jnp.max(chk[...]) <= PLAIN

        @pl.when(plain)
        def _():
            row_f[...] += row_t[...]
            if not diag:
                col_f[r, :, :width] += col_t[:, :width]

        @pl.when(jnp.logical_not(plain))
        def _():
            def group(g, _):
                at = pl.multiple_of(g * G, G)
                w = sc[pl.ds(at, G), :width] * GAIN
                old = row_m[pl.ds(at, G), :]
                top = jnp.maximum(old, lanes(w, jnp.maximum))
                total = row_s[pl.ds(at, G), :] * jnp.exp2(old - top)
                for k in range(width // 128):
                    total = total + jnp.exp2(w[:, k * 128 : (k + 1) * 128] - top)
                row_m[pl.ds(at, G), :] = top
                row_s[pl.ds(at, G), :] = total
                if not diag:
                    old = col_m[r, :, :width]
                    top = jnp.maximum(old, rows8(w, jnp.maximum))
                    total = col_s[r, :, :width] * jnp.exp2(old - top)
                    for k in range(G // 8):
                        total = total + jnp.exp2(w[k * 8 : (k + 1) * 8, :] - top)
                    col_m[r, :, :width] = top
                    col_s[r, :, :width] = total
                return 0

            lax.fori_loop(0, B // G, group, 0)

    def arrive(r):
        @pl.when(waited[r] == 0)
        def _():
            for s in range(nr):

                @pl.when(r == s)
                def _(s=s):
                    for c in copies(1, s):
                        c.wait()

            waited[r] = 1

    def runs():
        start = 0
        for r in range(1, nr + 1):
            if r == nr or widths[r] != widths[start]:
                yield start, r, widths[start]
                start = r

    def left(q, _):
        needed = functools.reduce(jnp.logical_or, [live[q * nr + r] > 0 for r in range(nr)])
        row_out[pl.ds(q, 1), :] = jnp.full((1, B), FLOOR, jnp.float32)

        @pl.when(needed)
        def _():
            row_f[...] = jnp.zeros_like(row_f)
            row_s[...] = jnp.zeros_like(row_s)
            row_m[...] = jnp.full_like(row_m, FLOOR)
            for s in range(nl):

                @pl.when(q == s)
                def _(s=s):
                    for c in copies(0, s):
                        c.wait()

            if own_first:

                @pl.when(q == 0)
                def _():
                    arrive(0)
                    pair(0, 0, B, True)

            for start, stop, width in runs():

                def step(r, _, width=width):
                    go = live[q * nr + r] > 0
                    if own_first:
                        go = jnp.logical_and(go, q + r > 0)

                    @pl.when(go)
                    def _():
                        arrive(r)
                        pair(q, r, width, False)

                    return 0

                lax.fori_loop(start, stop, step, 0)
            row_out[pl.ds(q, 1), :] = fold(row_m[...].T, row_s[...].T, row_f[...].T, 0)

        return 0

    lax.fori_loop(0, nl, left, 0)
    for r in range(nr):
        col_out[r : r + 1, :] = jnp.full((1, B), FLOOR, jnp.float32)

        @pl.when(need_r[r])
        def _(r=r):
            col_out[r : r + 1, :] = fold(col_m[r], col_s[r], col_f[r], 0)

    for out, prevs in ((row_out, row_prev), (col_out, col_prev)):
        at = 0
        for prev in prevs:
            to = at + prev.shape[0]
            out[at:to, :] = log2_add(out[at:to, :], prev[...])
            at = to

    if last:
        ring_out, next_out, after_out = outs
        chip, core = live[nl * nr], live[nl * nr + 1]
        for q in range(nl):
            at = (chip + PLACES[q][0]) % 4 * 2 + (core + PLACES[q][1]) % 2
            row = row_out[q : q + 1, :]
            ring_out[at] = row if q else log2_add(row, col_out[0:1, :])
        next_out[...] = col_out[1:2, :]
        after_out[:, : B // 2] = col_out[3:4, : B // 2]
        after_out[:, B // 2 :] = col_out[2:3, : B // 2]


def stage(name, live, lefts, rights, row_prev=(), col_prev=(), own_first=False, last=False):
    nl, nr = len(lefts), len(rights)
    flat, tables = [], []
    for side in (lefts, rights):
        table = []
        for slot, pieces in enumerate(side):
            for array, src, dst, count in pieces:
                flat.append(array)
                table.append((slot, src, dst, count))
        tables.append(tuple(table))
    widths = tuple(sum(piece[3] for piece in pieces) for pieces in rights)
    nrow, ncol = tuple(p.shape[0] for p in row_prev), tuple(p.shape[0] for p in col_prev)
    plan = (nl, nr, tables[0], tables[1], widths, nrow, ncol, own_first, last)
    f32 = jnp.float32
    shapes = [(RING, 1, B), (1, B), (1, B)] if last else [(nl, B), (nr, B)]
    shapes = [jax.ShapeDtypeStruct(shape, f32) for shape in shapes]
    return pl.pallas_call(
        functools.partial(stage_kernel, plan),
        out_shape=shapes,
        in_specs=[pl.BlockSpec(memory_space=pltpu.SMEM)]
        + [pl.BlockSpec(memory_space=pltpu.VMEM)] * (len(nrow) + len(ncol))
        + [pl.BlockSpec(memory_space=pl.ANY)] * len(flat),
        out_specs=[pl.BlockSpec(memory_space=pltpu.VMEM)] * len(shapes),
        scratch_shapes=[
            pltpu.VMEM((nl, B, D), jnp.bfloat16),
            pltpu.VMEM((nr, B, D), jnp.bfloat16),
            pltpu.VMEM((B, B), f32),
            pltpu.VMEM((B, 128), f32),
            pltpu.VMEM((8, B), f32),
            pltpu.VMEM((8, 128), f32),
            pltpu.VMEM((B, 128), f32),
            pltpu.VMEM((B, 128), f32),
            pltpu.VMEM((B, 128), f32),
            pltpu.VMEM((nr, 8, B), f32),
            pltpu.VMEM((nr, 8, B), f32),
            pltpu.VMEM((nr, 8, B), f32),
            pltpu.SMEM((nr,), jnp.int32),
            pltpu.SemaphoreType.DMA((nl,)),
            pltpu.SemaphoreType.DMA((nr,)),
            pltpu.VMEM((nl, B), f32),
            pltpu.VMEM((nr, B), f32),
        ],
        compiler_params=pltpu.CompilerParams(vmem_limit_bytes=GRANT),
        cost_estimate=pl.CostEstimate(
            flops=2 * B * B * D * max(1, nl * nr // 4), bytes_accessed=2 * B * D * (nl + nr), transcendentals=0
        ),
        name=name,
    )(live, *row_prev, *col_prev, *flat)


def last_kernel(row_ref, ring_ref, *refs):
    parts, o_ref = refs[:-1], refs[-1]
    row = row_ref[0]
    got = [ring_ref[k] for k in range(RING)]
    for k, part in enumerate(parts):
        got.append(jnp.where(row > k, part[...], FLOOR))
    got = jnp.concatenate(got, 0)
    best = jnp.max(got, 0, keepdims=True)
    total = jnp.sum(jnp.exp2(got - best), 0, keepdims=True)
    o_ref[...] = (best + jnp.log2(total)) * (LN2 / SCALE)


def body(embeddings, partners, pair_count):
    unit, top, low = normalize(embeddings, partners, pair_count)
    me = lax.axis_index("dp")
    column = me % RING
    swap = along(0, 1)

    a = send(unit, around(1))
    b = send(unit, around(-1))
    c = send(unit, along(-RING))
    over, on = [], []
    for d in range(2 * RING, COUNT):
        z, y = d // 32, (d // RING) % 4
        relay = (z - (y < 2)) * 32 + (y + 1) % 4 * RING + d % RING
        over.append((d, relay))
        on.append((relay, d - 2 * RING))
    relayed = send(low, over)
    sib = send(unit, swap)

    targets = me + RING * jnp.array([0, 1, 2, 2], jnp.int32)

    def pairs_of(*arrays):
        lists = jnp.concatenate([x[-LIST : 1 - LIST, :16] for x in arrays], 0).astype(jnp.int32)
        return jnp.any(lists[:, None, :] == targets[None, :, None], -1).astype(jnp.int32)

    def whole(array):
        return [(array, 0, 0, B)]

    rights = [whole(unit)]
    row_0, _ = stage("own", jnp.ones((1,), jnp.int32), rights, rights, own_first=True)
    relayed, sib, row_0 = lax.optimization_barrier((relayed, sib, row_0))
    d_low = send(relayed, on)
    sib_pairs = pairs_of(sib)
    row_1, col_1 = stage("sibling", sib_pairs[0, :1], [whole(sib)], rights)
    a, b, c, d_low, row_1 = lax.optimization_barrier((a, b, c, d_low, row_1))

    a_top, b_low = halves(a, b)
    f_top = send(a_top, around(1))
    f_low = send(b_low, around(-1))
    top, a, b, a_top = lax.optimization_barrier((top, a, b, a_top))
    d_top = send(top, along(-2 * RING))
    a_sib = send(a, swap)
    b_sib = send(b, swap)

    rights = rights + [whole(c), [(d_low, 0, 0, H)]]
    early = jnp.concatenate([pairs_of(unit), sib_pairs, pairs_of(a, b)], 0)
    live = early.at[:2, :1].set(0)[:, :3]
    lefts = [whole(unit), whole(sib), whole(a), whole(b)]
    row_2, col_2 = stage("near", live.reshape(-1), lefts, rights, [row_0, row_1], [col_1])
    a_sib, b_sib, row_2 = lax.optimization_barrier((a_sib, b_sib, row_2))
    more = pairs_of(a_sib, b_sib)
    row_3, col_3 = stage("mid", more[:, :3].reshape(-1), [whole(a_sib), whole(b_sib)], rights, [], [col_2])
    f_top, f_low, d_top, row_3 = lax.optimization_barrier((f_top, f_low, d_top, row_3))
    f_top_sib = send(f_top, swap)
    f_low_sib = send(f_low, swap)

    rights = rights + [[(d_top, 0, 0, H)]]
    lefts = lefts + [whole(a_sib), whole(b_sib)]
    lefts = lefts + [[(f_top, 0, 0, H), (f_low, 0, H, H)], [(f_top_sib, 0, 0, H), (f_low_sib, 0, H, H)]]
    early = jnp.concatenate([early, more], 0).at[:, :3].set(0)
    live = jnp.concatenate([early, pairs_of(f_low, f_low_sib)], 0)
    place = jnp.stack([column // 2, column % 2]).astype(jnp.int32)
    live = jnp.concatenate([live.reshape(-1), place])
    ring_part, next_part, after_part = stage("far", live, lefts, rights, [row_2, row_3], [col_3], last=True)

    next_got = send(next_part, along(RING))
    after_got = send(after_part, along(2 * RING))
    groups = [[r * RING + k for k in range(RING)] for r in range(COUNT // RING)]
    ring_got = lax.all_to_all(ring_part, "dp", 0, 0, axis_index_groups=groups, tiled=True)
    out = pl.pallas_call(
        last_kernel,
        in_specs=[pl.BlockSpec(memory_space=pltpu.SMEM)] + [pl.BlockSpec(memory_space=pltpu.VMEM)] * 3,
        out_shape=jax.ShapeDtypeStruct((1, B), jnp.float32),
        name="last_sum",
    )((me // RING)[None].astype(jnp.int32), ring_got, next_got, after_got)
    return out.reshape(B)


def solution(mesh):
    placed = (P("dp", None), P("dp", None), P("dp"))
    return jax.shard_map(body, mesh=mesh, in_specs=placed, out_specs=P("dp"), check_vma=False)
```

profile of v0, /device:TPU:34, one launch (start us, length us, event | category | flops | bytes accessed | tf_op | source)
XLA Modules:
  0.0 143.1 jit_solution(8650658907986231630)
XLA Ops:
  0.7 4.1 %unit_rows.1 = (bf16[1040,1024]{1,0:T(8,128)(2,1)}, bf16[512,1024]{1,0:T(8,128)(2,1)}, bf16[512,1024]{1,0:T(8,128)(2,1)}) custom-call(s32[1,13]{1,0:T(1,128)} %list_ref.1, s32[1]{0:T(128)S(6)} %copy.7.count_ref, bf16[1024,1024]{1,0:T(8,128)(2,1)} %x_ref.1), custom_call_target="tpu_custom_call" | custom-call | tf_op jit(solution)/shard_map/unit_rows/pallas_call | solution.py:81
  4.8 0.1 collective-permute-start.1
  4.8 3.0 %collective-permute-start = (bf16[512,1024]{1,0:T(8,128)(2,1)}, bf16[512,1024]{1,0:T(8,128)(2,1)S(1)}, u32[]{:S(2)}, u32[]{:S(2)}) collective-permute-start(bf16[512,1024]{1,0:T(8,128)(2,1)} %get-tuple-element.63), channel_id=1, source_target_pairs={{16,24},{17,25},{18,26},{19,27},{20,28},{21,29},{22,30},{23,31},{2... | collective-permute-start | bytes 3145736 | tf_op jit(solution)/shard_map/ppermute | solution.py:44
  7.9 3.6 %collective-permute-start.4 = (bf16[1040,1024]{1,0:T(8,128)(2,1)}, bf16[1040,1024]{1,0:T(8,128)(2,1)}, u32[]{:S(2)}, u32[]{:S(2)}) collective-permute-start(bf16[1040,1024]{1,0:T(8,128)(2,1)} %get-tuple-element.62.refs_0_.refs_1_.refs_3_.refs_7_.refs_13_), channel_id=1, source_target_pairs={{8,0},{9,1},{10,2},{11,3},{12,4},{13,5},{14,6},{15,7},{16,8},{17,9... | collective-permute-start | bytes 6389768 | tf_op jit(solution)/shard_map/ppermute | solution.py:44
  11.5 0.5 collective-permute-start.3
  12.0 1.6 %collective-permute-start.2 = (bf16[1040,1024]{1,0:T(8,128)(2,1)}, bf16[1040,1024]{1,0:T(8,128)(2,1)}, u32[]{:S(2)}, u32[]{:S(2)}) collective-permute-start(bf16[1040,1024]{1,0:T(8,128)(2,1)} %get-tuple-element.62.refs_0_.refs_1_.refs_3_.refs_7_.refs_13_), channel_id=1, source_target_pairs={{0,2},{1,3},{2,4},{3,5},{4,6},{5,7},{6,0},{7,1},{8,10},{9,11},{10,... | collective-permute-start | bytes 6389768 | tf_op jit(solution)/shard_map/ppermute | solution.py:44
  13.6 7.5 %own.1 = (f32[1,1024]{1,0:T(1,128)}, f32[1,1024]{1,0:T(1,128)}) custom-call(s32[1]{0:T(128)} %constant.106.clone.1.live, bf16[1040,1024]{1,0:T(8,128)(2,1)} %get-tuple-element.62.refs_0_.refs_1_.refs_3_.refs_7_.refs_13_, bf16[1040,1024]{1,0:T(8,128)(2,1)} %get-tuple-element.62.refs_0_.refs_1_.refs_3_.refs_7_.refs_13_), custom_call_target="tpu_custom_call" | custom-call | flops 2147483648 | bytes 4194304 | tf_op jit(solution)/shard_map/own/pallas_call | solution.py:375
  21.1 12.7 %collective-permute-done = bf16[512,1024]{1,0:T(8,128)(2,1)S(1)} collective-permute-done((bf16[512,1024]{1,0:T(8,128)(2,1)}, bf16[512,1024]{1,0:T(8,128)(2,1)S(1)}, u32[]{:S(2)}, u32[]{:S(2)}) %collective-permute-start) | collective-permute-done | bytes 1048608 | tf_op jit(solution)/shard_map/ppermute | solution.py:44
  33.8 0.0 collective-permute-done.1.refs_0_.refs_4_
  33.8 1.0 copy-done.7
  34.8 3.1 %collective-permute-start.5 = (bf16[512,1024]{1,0:T(8,128)(2,1)}, bf16[512,1024]{1,0:T(8,128)(2,1)S(1)}, u32[]{:S(2)}, u32[]{:S(2)}) collective-permute-start(bf16[512,1024]{1,0:T(8,128)(2,1)} %copy-done.7), channel_id=1, source_target_pairs={{24,0},{25,1},{26,2},{27,3},{28,4},{29,5},{30,6},{31,7},{0,8},{1,9... | collective-permute-start | bytes 3145736 | tf_op jit(solution)/shard_map/ppermute | solution.py:44
  37.9 0.0 copy-done.8
  37.9 0.7 bitcast_convert_fusion.1
  38.6 0.7 bitcast_convert_fusion
  39.3 0.2 compare_reduce_fusion.4
  39.5 0.5 convert_bitcast_fusion
  40.0 1.3 sibling.1
  41.3 17.3 %collective-permute-done.4.refs_8_.refs_4_.refs_14_ = bf16[1040,1024]{1,0:T(8,128)(2,1)} collective-permute-done((bf16[1040,1024]{1,0:T(8,128)(2,1)}, bf16[1040,1024]{1,0:T(8,128)(2,1)}, u32[]{:S(2)}, u32[]{:S(2)}) %collective-permute-start.4) | collective-permute-done | bytes 2129952 | tf_op jit(solution)/shard_map/ppermute | solution.py:44
  58.5 1.5 %collective-permute-done.3.b_ref.refs_6_ = bf16[1040,1024]{1,0:T(8,128)(2,1)} collective-permute-done((bf16[1040,1024]{1,0:T(8,128)(2,1)}, bf16[1040,1024]{1,0:T(8,128)(2,1)}, u32[]{:S(2)}, u32[]{:S(2)}) %collective-permute-start.3) | collective-permute-done | bytes 2129952 | tf_op jit(solution)/shard_map/ppermute | solution.py:44
  60.1 1.3 collective-permute-done.2.a_ref.refs_5_
  61.4 1.5 %collective-permute-done.5.refs_9_.refs_5_.refs_15_ = bf16[512,1024]{1,0:T(8,128)(2,1)S(1)} collective-permute-done((bf16[512,1024]{1,0:T(8,128)(2,1)}, bf16[512,1024]{1,0:T(8,128)(2,1)S(1)}, u32[]{:S(2)}, u32[]{:S(2)}) %collective-permute-start.5) | collective-permute-done | bytes 1048608 | tf_op jit(solution)/shard_map/ppermute | solution.py:44
  62.9 2.8 %halves.1 = (bf16[512,1024]{1,0:T(8,128)(2,1)}, bf16[528,1024]{1,0:T(8,128)(2,1)}) custom-call(bf16[1040,1024]{1,0:T(8,128)(2,1)} %collective-permute-done.2.a_ref.refs_5_, bf16[1040,1024]{1,0:T(8,128)(2,1)} %collective-permute-done.3.b_ref.refs_6_), custom_call_target="tpu_custom_call" | custom-call | tf_op jit(solution)/shard_map/halves/pallas_call | solution.py:121
  65.7 0.1 collective-permute-start.6
  65.8 0.5 collective-permute-start.7
  66.3 0.7 slice.75
  67.0 0.7 slice.76
  67.7 1.5 %collective-permute-start.8 = (bf16[512,1024]{1,0:T(8,128)(2,1)}, bf16[512,1024]{1,0:T(8,128)(2,1)S(1)}, u32[]{:S(2)}, u32[]{:S(2)}) collective-permute-start(bf16[512,1024]{1,0:T(8,128)(2,1)} %get-tuple-element.71), channel_id=1, source_target_pairs={{0,2},{1,3},{2,4},{3,5},{4,6},{5,7},{6,0},{7,1},{8,10},{9,11},{10,... | collective-permute-start | bytes 3145736 | tf_op jit(solution)/shard_map/ppermute | solution.py:44
  69.2 0.2 compare_reduce_fusion.2
  69.4 3.0 %collective-permute-start.10 = (bf16[512,1024]{1,0:T(8,128)(2,1)}, bf16[512,1024]{1,0:T(8,128)(2,1)}, u32[]{:S(2)}, u32[]{:S(2)}) collective-permute-start(bf16[512,1024]{1,0:T(8,128)(2,1)} %get-tuple-element.83), channel_id=1, source_target_pairs={{16,0},{17,1},{18,2},{19,3},{20,4},{21,5},{22,6},{23,7},{24,8},{25... | collective-permute-start | bytes 3145736 | tf_op jit(solution)/shard_map/ppermute | solution.py:44
  72.3 0.8 collective-permute-start.9
  73.1 0.0 copy-done.2
  73.2 0.2 scatter.6
  73.3 0.6 reshape.231.live
  73.9 12.4 %near.1 = (f32[4,1024]{1,0:T(4,128)}, f32[3,1024]{1,0:T(4,128)}) custom-call(s32[12]{0:T(128)} %reshape.231.live, f32[1,1024]{1,0:T(1,128)} %get-tuple-element.74.refs_0_, f32[1,1024]{1,0:T(1,128)} %get-tuple-element.75.refs_1_, f32[1,1024]{1,0:T(1,128)} %get-tuple-element.76.refs_2_, ...), custom_call_target="tpu_custom_call" | custom-call | flops 6442450944 | bytes 14680064 | tf_op jit(solution)/shard_map/near/pallas_call | solution.py:375
  86.3 0.0 collective-permute-done.6.refs_1_.refs_7_
  86.3 0.0 collective-permute-done.7.refs_2_.refs_8_
  86.3 0.7 slice.78
  87.0 0.7 slice.79
  87.6 0.2 compare_reduce_fusion.1
  87.8 0.6 reshape.232.live
  88.4 1.4 %mid.1 = (f32[2,1024]{1,0:T(2,128)}, f32[3,1024]{1,0:T(4,128)}) custom-call(s32[6]{0:T(128)} %reshape.232.live, f32[3,1024]{1,0:T(4,128)} %get-tuple-element.84.refs_0_, bf16[1040,1024]{1,0:T(8,128)(2,1)} %collective-permute-done.6.refs_1_.refs_7_, bf16[1040,1024]{1,0:T(8,128)(2,1)} %collective-permute-done.7.refs_2_.refs_8_, ...), custom_call_target="tpu_custom_call" | custom-call | flops 2147483648 | bytes 10485760 | tf_op jit(solution)/shard_map/mid/pallas_call | solution.py:375
  89.9 8.1 %collective-permute-done.10.refs_16_ = bf16[512,1024]{1,0:T(8,128)(2,1)} collective-permute-done((bf16[512,1024]{1,0:T(8,128)(2,1)}, bf16[512,1024]{1,0:T(8,128)(2,1)}, u32[]{:S(2)}, u32[]{:S(2)}) %collective-permute-start.10) | collective-permute-done | bytes 1048608 | tf_op jit(solution)/shard_map/ppermute | solution.py:44
  98.0 0.0 collective-permute-done.8.refs_9_
  98.0 0.3 collective-permute-done.9.refs_10_
  98.2 0.0 collective-permute-start.11
  98.2 0.5 collective-permute-start.12
  98.7 0.7 slice.81
  99.4 0.2 scatter.9
  99.6 1.6 %collective-permute-done.11.refs_12_ = bf16[528,1024]{1,0:T(8,128)(2,1)S(1)} collective-permute-done((bf16[528,1024]{1,0:T(8,128)(2,1)}, bf16[528,1024]{1,0:T(8,128)(2,1)S(1)}, u32[]{:S(2)}, u32[]{:S(2)}) %collective-permute-start.11) | collective-permute-done | bytes 1081376 | tf_op jit(solution)/shard_map/ppermute | solution.py:44
  101.2 1.0 copy-done.5
  102.2 0.2 compare_reduce_fusion
  102.4 0.1 reshape.233
  102.5 0.6 pad_add_fusion.3.live
  103.1 0.0 collective-permute-done.12.refs_11_
  103.1 12.6 %far.1 = (f32[8,1,1024]{2,1,0:T(1,128)}, f32[1,1024]{1,0:T(1,128)}, f32[1,1024]{1,0:T(1,128)}) custom-call(s32[34]{0:T(128)} %pad_add_fusion.3.live, f32[4,1024]{1,0:T(4,128)} %get-tuple-element.87.refs_0_, f32[2,1024]{1,0:T(2,128)} %get-tuple-element.88.refs_1_, f32[3,1024]{1,0:T(4,128)} %get-tuple-element.89.refs_2_, ...), custom_call_target="tpu_custom_call" | custom-call | flops 17179869184 | bytes 25165824 | tf_op jit(solution)/shard_map/far/pallas_call | solution.py:375
  115.8 10.2 %all-to-all-start = ((f32[8,1,1024]{2,1,0:T(1,128)}), f32[8,1,1024]{2,1,0:T(1,128)S(1)}, u32[]{:S(2)}, u32[]{:S(2)}) async-start(f32[8,1,1024]{2,1,0:T(1,128)} %get-tuple-element.92), calls=%async_computation | async-start | bytes 65536 | tf_op jit(solution)/shard_map/all_to_all | solution.py:488
  125.9 7.0 %collective-permute-start.13 = (f32[1,1024]{1,0:T(1,128)}, f32[1,1024]{1,0:T(1,128)S(1)}, u32[]{:S(2)}, u32[]{:S(2)}) collective-permute-start(f32[1,1024]{1,0:T(1,128)} %get-tuple-element.93), channel_id=1, source_target_pairs={{0,8},{1,9},{2,10},{3,11},{4,12},{5,13},{6,14},{7,15},{8,16},{9,17... | collective-permute-start | bytes 12296 | tf_op jit(solution)/shard_map/ppermute | solution.py:44
  133.0 1.9 %collective-permute-start.14 = (f32[1,1024]{1,0:T(1,128)}, f32[1,1024]{1,0:T(1,128)S(1)}, u32[]{:S(2)}, u32[]{:S(2)}) collective-permute-start(f32[1,1024]{1,0:T(1,128)} %get-tuple-element.94), channel_id=1, source_target_pairs={{0,16},{1,17},{2,18},{3,19},{4,20},{5,21},{6,22},{7,23},{8,24},{9,... | collective-permute-start | bytes 12296 | tf_op jit(solution)/shard_map/ppermute | solution.py:44
  134.9 0.0 collective-permute-done.13.refs_0_
  134.9 6.2 %collective-permute-done.14.refs_1_ = f32[1,1024]{1,0:T(1,128)S(1)} collective-permute-done((f32[1,1024]{1,0:T(1,128)}, f32[1,1024]{1,0:T(1,128)S(1)}, u32[]{:S(2)}, u32[]{:S(2)}) %collective-permute-start.14) | collective-permute-done | bytes 4128 | tf_op jit(solution)/shard_map/ppermute | solution.py:44
  141.1 0.0 all-to-all-done.ring_ref
  141.1 0.6 copy-done.4
  141.7 0.0 copy-done.1
  141.7 1.4 last_sum.1
  (25 shorter events, 0.1 us)
Async XLA Ops:
  4.8 29.0 %collective-permute-start.1 = (bf16[1040,1024]{1,0:T(8,128)(2,1)}, bf16[1040,1024]{1,0:T(8,128)(2,1)}, u32[]{:S(2)}, u32[]{:S(2)}) collective-permute-start(bf16[1040,1024]{1,0:T(8,128)(2,1)} %get-tuple-element.62.refs_0_.refs_1_.refs_3_.refs_7_.refs_13_), channel_id=1, source_target_pairs={{0,1},{1,0},{2,3},{3,2},{4,5},{5,4},{6,7},{7,6},{8,9},{9,8},{10,11... | collective-permute-start | bytes 6389768 | tf_op jit(solution)/shard_map/ppermute | solution.py:44
  4.8 28.9 %collective-permute-start = (bf16[512,1024]{1,0:T(8,128)(2,1)}, bf16[512,1024]{1,0:T(8,128)(2,1)S(1)}, u32[]{:S(2)}, u32[]{:S(2)}) collective-permute-start(bf16[512,1024]{1,0:T(8,128)(2,1)} %get-tuple-element.63), channel_id=1, source_target_pairs={{16,24},{17,25},{18,26},{19,27},{20,28},{21,29},{22,30},{23,31},{2... | collective-permute-start | bytes 3145736 | tf_op jit(solution)/shard_map/ppermute | solution.py:44
  7.9 50.7 %collective-permute-start.4 = (bf16[1040,1024]{1,0:T(8,128)(2,1)}, bf16[1040,1024]{1,0:T(8,128)(2,1)}, u32[]{:S(2)}, u32[]{:S(2)}) collective-permute-start(bf16[1040,1024]{1,0:T(8,128)(2,1)} %get-tuple-element.62.refs_0_.refs_1_.refs_3_.refs_7_.refs_13_), channel_id=1, source_target_pairs={{8,0},{9,1},{10,2},{11,3},{12,4},{13,5},{14,6},{15,7},{16,8},{17,9... | collective-permute-start | bytes 6389768 | tf_op jit(solution)/shard_map/ppermute | solution.py:44
  11.5 48.6 %collective-permute-start.3 = (bf16[1040,1024]{1,0:T(8,128)(2,1)}, bf16[1040,1024]{1,0:T(8,128)(2,1)}, u32[]{:S(2)}, u32[]{:S(2)}) collective-permute-start(bf16[1040,1024]{1,0:T(8,128)(2,1)} %get-tuple-element.62.refs_0_.refs_1_.refs_3_.refs_7_.refs_13_), channel_id=1, source_target_pairs={{0,6},{1,7},{2,0},{3,1},{4,2},{5,3},{6,4},{7,5},{8,14},{9,15},{10,... | collective-permute-start | bytes 6389768 | tf_op jit(solution)/shard_map/ppermute | solution.py:44
  12.0 49.4 %collective-permute-start.2 = (bf16[1040,1024]{1,0:T(8,128)(2,1)}, bf16[1040,1024]{1,0:T(8,128)(2,1)}, u32[]{:S(2)}, u32[]{:S(2)}) collective-permute-start(bf16[1040,1024]{1,0:T(8,128)(2,1)} %get-tuple-element.62.refs_0_.refs_1_.refs_3_.refs_7_.refs_13_), channel_id=1, source_target_pairs={{0,2},{1,3},{2,4},{3,5},{4,6},{5,7},{6,0},{7,1},{8,10},{9,11},{10,... | collective-permute-start | bytes 6389768 | tf_op jit(solution)/shard_map/ppermute | solution.py:44
  13.6 24.3 %copy-start.8 = (s32[4]{0:T(128)S(1)}, s32[4]{0:T(128)}, u32[]{:S(2)}) copy-start(s32[4]{0:T(128)} %constant.111) | copy-start | bytes 52
  33.8 1.0 copy-start.7
  34.8 28.1 %collective-permute-start.5 = (bf16[512,1024]{1,0:T(8,128)(2,1)}, bf16[512,1024]{1,0:T(8,128)(2,1)S(1)}, u32[]{:S(2)}, u32[]{:S(2)}) collective-permute-start(bf16[512,1024]{1,0:T(8,128)(2,1)} %copy-done.7), channel_id=1, source_target_pairs={{24,0},{25,1},{26,2},{27,3},{28,4},{29,5},{30,6},{31,7},{0,8},{1,9... | collective-permute-start | bytes 3145736 | tf_op jit(solution)/shard_map/ppermute | solution.py:44
  62.9 2.8 %copy-start = (bf16[512,1024]{1,0:T(8,128)(2,1)}, bf16[512,1024]{1,0:T(8,128)(2,1)S(1)}, u32[]{:S(2)}) copy-start(bf16[512,1024]{1,0:T(8,128)(2,1)S(1)} %collective-permute-done.5.refs_9_.refs_5_.refs_15_) | copy-start | bytes 3145732
  62.9 10.2 %copy-start.2 = (s32[1,4]{1,0:T(1,128)S(1)}, s32[1,4]{1,0:T(1,128)}, u32[]{:S(2)}) copy-start(s32[1,4]{1,0:T(1,128)} %get-tuple-element.97) | copy-start | bytes 52
  65.7 20.5 %collective-permute-start.6 = (bf16[1040,1024]{1,0:T(8,128)(2,1)}, bf16[1040,1024]{1,0:T(8,128)(2,1)}, u32[]{:S(2)}, u32[]{:S(2)}) collective-permute-start(bf16[1040,1024]{1,0:T(8,128)(2,1)} %collective-permute-done.2.a_ref.refs_5_), channel_id=1, source_target_pairs={{0,1},{1,0},{2,3},{3,2},{4,5},{5,4},{6,7},{7,6},{8,9},{9,8},{10,11... | collective-permute-start | bytes 6389768 | tf_op jit(solution)/shard_map/ppermute | solution.py:44
  65.8 20.5 %collective-permute-start.7 = (bf16[1040,1024]{1,0:T(8,128)(2,1)}, bf16[1040,1024]{1,0:T(8,128)(2,1)}, u32[]{:S(2)}, u32[]{:S(2)}) collective-permute-start(bf16[1040,1024]{1,0:T(8,128)(2,1)} %collective-permute-done.3.b_ref.refs_6_), channel_id=1, source_target_pairs={{0,1},{1,0},{2,3},{3,2},{4,5},{5,4},{6,7},{7,6},{8,9},{9,8},{10,11... | collective-permute-start | bytes 6389768 | tf_op jit(solution)/shard_map/ppermute | solution.py:44
  67.7 30.3 %collective-permute-start.8 = (bf16[512,1024]{1,0:T(8,128)(2,1)}, bf16[512,1024]{1,0:T(8,128)(2,1)S(1)}, u32[]{:S(2)}, u32[]{:S(2)}) collective-permute-start(bf16[512,1024]{1,0:T(8,128)(2,1)} %get-tuple-element.71), channel_id=1, source_target_pairs={{0,2},{1,3},{2,4},{3,5},{4,6},{5,7},{6,0},{7,1},{8,10},{9,11},{10,... | collective-permute-start | bytes 3145736 | tf_op jit(solution)/shard_map/ppermute | solution.py:44
  69.4 28.6 %collective-permute-start.10 = (bf16[512,1024]{1,0:T(8,128)(2,1)}, bf16[512,1024]{1,0:T(8,128)(2,1)}, u32[]{:S(2)}, u32[]{:S(2)}) collective-permute-start(bf16[512,1024]{1,0:T(8,128)(2,1)} %get-tuple-element.83), channel_id=1, source_target_pairs={{16,0},{17,1},{18,2},{19,3},{20,4},{21,5},{22,6},{23,7},{24,8},{25... | collective-permute-start | bytes 3145736 | tf_op jit(solution)/shard_map/ppermute | solution.py:44
  72.3 25.9 %collective-permute-start.9 = (bf16[528,1024]{1,0:T(8,128)(2,1)}, bf16[528,1024]{1,0:T(8,128)(2,1)}, u32[]{:S(2)}, u32[]{:S(2)}) collective-permute-start(bf16[528,1024]{1,0:T(8,128)(2,1)} %get-tuple-element.82), channel_id=1, source_target_pairs={{0,6},{1,7},{2,0},{3,1},{4,2},{5,3},{6,4},{7,5},{8,14},{9,15},{10,... | collective-permute-start | bytes 3244040 | tf_op jit(solution)/shard_map/ppermute | solution.py:44
  98.0 5.2 %copy-start.6 = (bf16[512,1024]{1,0:T(8,128)(2,1)}, bf16[512,1024]{1,0:T(8,128)(2,1)S(1)}, u32[]{:S(2)}) copy-start(bf16[512,1024]{1,0:T(8,128)(2,1)S(1)} %collective-permute-done.8.refs_9_) | copy-start | bytes 3145732
  98.2 3.0 %collective-permute-start.11 = (bf16[528,1024]{1,0:T(8,128)(2,1)}, bf16[528,1024]{1,0:T(8,128)(2,1)S(1)}, u32[]{:S(2)}, u32[]{:S(2)}) collective-permute-start(bf16[528,1024]{1,0:T(8,128)(2,1)} %collective-permute-done.9.refs_10_), channel_id=1, source_target_pairs={{0,1},{1,0},{2,3},{3,2},{4,5},{5,4},{6,7},{7,6},{8,9},{9,8},{10,11... | collective-permute-start | bytes 3244040 | tf_op jit(solution)/shard_map/ppermute | solution.py:44
  98.2 4.9 %collective-permute-start.12 = (bf16[512,1024]{1,0:T(8,128)(2,1)S(1)}, bf16[512,1024]{1,0:T(8,128)(2,1)}, u32[]{:S(2)}, u32[]{:S(2)}) collective-permute-start(bf16[512,1024]{1,0:T(8,128)(2,1)S(1)} %collective-permute-done.8.refs_9_), channel_id=1, source_target_pairs={{0,1},{1,0},{2,3},{3,2},{4,5},{5,4},{6,7},{7,6},{8,9},{9,8},{10,11... | collective-permute-start | bytes 3145736 | tf_op jit(solution)/shard_map/ppermute | solution.py:44
  101.2 1.0 copy-start.5
  115.8 25.3 %all-to-all-start = ((f32[8,1,1024]{2,1,0:T(1,128)}), f32[8,1,1024]{2,1,0:T(1,128)S(1)}, u32[]{:S(2)}, u32[]{:S(2)}) async-start(f32[8,1,1024]{2,1,0:T(1,128)} %get-tuple-element.92), calls=%async_computation | async-start | bytes 65536 | tf_op jit(solution)/shard_map/all_to_all | solution.py:488
  125.9 9.0 %collective-permute-start.13 = (f32[1,1024]{1,0:T(1,128)}, f32[1,1024]{1,0:T(1,128)S(1)}, u32[]{:S(2)}, u32[]{:S(2)}) collective-permute-start(f32[1,1024]{1,0:T(1,128)} %get-tuple-element.93), channel_id=1, source_target_pairs={{0,8},{1,9},{2,10},{3,11},{4,12},{5,13},{6,14},{7,15},{8,16},{9,17... | collective-permute-start | bytes 12296 | tf_op jit(solution)/shard_map/ppermute | solution.py:44
  133.0 8.1 %collective-permute-start.14 = (f32[1,1024]{1,0:T(1,128)}, f32[1,1024]{1,0:T(1,128)S(1)}, u32[]{:S(2)}, u32[]{:S(2)}) collective-permute-start(f32[1,1024]{1,0:T(1,128)} %get-tuple-element.94), channel_id=1, source_target_pairs={{0,16},{1,17},{2,18},{3,19},{4,20},{5,21},{6,22},{7,23},{8,24},{9,... | collective-permute-start | bytes 12296 | tf_op jit(solution)/shard_map/ppermute | solution.py:44
  134.9 6.2 %copy-start.3 = (f32[1,1024]{1,0:T(1,128)}, f32[1,1024]{1,0:T(1,128)S(1)}, u32[]{:S(2)}) copy-start(f32[1,1024]{1,0:T(1,128)S(1)} %collective-permute-done.13.refs_0_) | copy-start | bytes 12292
  141.1 0.6 copy-start.4
  141.1 0.6 copy-start.1
where the time goes:
time: 144 us; the launch traced here: 143 us
  waiting for transfers between devices  50.4 us (35%)
  Pallas kernels  43.6 us (30%)
  starting transfers between devices  37.3 us (26%)
  local copies, waits for them, and re-layouts  7.53 us (5%)
  other arithmetic  3.35 us (2%)
    ppermute x15, waiting for transfers between devices, send(): return lax.ppermute(value, 'dp', moves)  50.4 us
    pallas_call x5, Pallas kernels, stage(): pl.pallas_call(functools.partial(stage_kernel, plan), out_shape=shapes, i...  35.2 us
    ppermute x15, starting transfers between devices, send(): return lax.ppermute(value, 'dp', moves)  27.2 us
    all_to_all x1, starting transfers between devices, body(): lax.all_to_all(ring_part, 'dp', 0, 0, axis_index_groups=groups, tiled=True)  10.2 us
    pallas_call x1, Pallas kernels, normalize(): pl.pallas_call(unit_kernel, in_specs=[smem, smem, anywhere], out_specs=[a...  4.1 us
    slice x6, local copies, waits for them, and re-layouts, pairs_of(): x[-LIST:1 - LIST, :16]  3.35 us
  transfers between devices with their start and end apart: 16, of which 9 were waited for; matrix products, arithmetic and copies ran while one was open for 6% of the time, Pallas kernels for 16%

commit v1 on v0

--- a/solution.py
+++ b/solution.py
@@ -11,10 +11,11 @@
 LOG2E = 1.4426950408889634
 LN2 = 0.6931471805599453
 GAIN = SCALE * LOG2E
-PLAIN = 78.0 / SCALE
+LEAST = 2.0**-60
+MOST = 2.0**112
 FLOOR = -1e30
 MASKED = -1e27
-SCRATCH = 17
+SCRATCH = 18
 PLACES = [(0, 0), (0, 1), (3, 0), (1, 0), (3, 1), (1, 1), (2, 0), (2, 1)]
 B = 1024
 D = 1024
@@ -25,7 +26,7 @@
 RING = 8
 HALVES = B // 2 // CH
 LIST = 16
-GRANT = 62 * 2**20
+GRANT = 63 * 2**20 + 2**19
 
 
 def around(dx):
@@ -57,8 +58,12 @@
         entry = jnp.where(k < count_ref[0], list_ref[0, k], -1).astype(jnp.float32)
         pairs = jnp.where(lane == k, entry, pairs)
     o[B : B + LIST, :] = pairs.astype(jnp.bfloat16)
-    stores = [pltpu.make_async_copy(o.at[pl.ds(B, LIST), :], o_ref.at[pl.ds(B, LIST), :], out_sem.at[0])]
+    stores = [
+        pltpu.make_async_copy(o.at[pl.ds(B, LIST), :], o_ref.at[pl.ds(B, LIST), :], out_sem.at[0]),
+        pltpu.make_async_copy(o.at[pl.ds(B, LIST), :], low_ref.at[pl.ds(H, LIST), :], out_sem.at[2 * (B // CH) + 1]),
+    ]
     stores[0].start()
+    stores[1].start()
     for i in range(B // CH):
         loads[i].wait()
         for g in range(CH // G):
@@ -84,49 +89,18 @@
         out_specs=[anywhere] * 3,
         out_shape=[
             jax.ShapeDtypeStruct((B + LIST, D), bf16),
-            jax.ShapeDtypeStruct((B // 2, D), bf16),
-            jax.ShapeDtypeStruct((B // 2, D), bf16),
+            jax.ShapeDtypeStruct((H, D), bf16),
+            jax.ShapeDtypeStruct((H + LIST, D), bf16),
         ],
         scratch_shapes=[
             pltpu.VMEM((B, D), bf16),
             pltpu.VMEM((B + LIST, D), bf16),
             pltpu.SemaphoreType.DMA((B // CH,)),
-            pltpu.SemaphoreType.DMA((2 * (B // CH) + 1,)),
+            pltpu.SemaphoreType.DMA((2 * (B // CH) + 2,)),
         ],
         compiler_params=pltpu.CompilerParams(vmem_limit_bytes=GRANT),
         name="unit_rows",
     )(partners, pair_count, embeddings)
-
-
-def halves_kernel(a_ref, b_ref, top_ref, low_ref, buf, sem):
-    n = B // 2 // CH
-    moves = []
-    for i in range(2 * n):
-        count = CH + LIST if i == 2 * n - 1 else CH
-        src = a_ref.at[pl.ds(i * CH, count), :] if i < n else b_ref.at[pl.ds(i * CH, count), :]
-        dst = top_ref.at[pl.ds(i * CH, count), :] if i < n else low_ref.at[pl.ds((i - n) * CH, count), :]
-        held = buf.at[pl.ds(i * CH, count), :]
-        moves.append((pltpu.make_async_copy(src, held, sem.at[2 * i]), pltpu.make_async_copy(held, dst, sem.at[2 * i + 1])))
-    for load, _ in moves:
-        load.start()
-    for load, store in moves:
-        load.wait()
-        store.start()
-    for _, store in moves:
-        store.wait()
-
-
-def halves(a, b):
-    bf16, anywhere = jnp.bfloat16, pl.BlockSpec(memory_space=pl.ANY)
-    return pl.pallas_call(
-        halves_kernel,
-        in_specs=[anywhere] * 2,
-        out_specs=[anywhere] * 2,
-        out_shape=[jax.ShapeDtypeStruct((B // 2, D), bf16), jax.ShapeDtypeStruct((B // 2 + LIST, D), bf16)],
-        scratch_shapes=[pltpu.VMEM((B + LIST, D), bf16), pltpu.SemaphoreType.DMA((2 * B // CH,))],
-        compiler_params=pltpu.CompilerParams(vmem_limit_bytes=GRANT),
-        name="halves",
-    )(a, b)
 
 
 def lanes(value, op):
@@ -157,7 +131,7 @@
     blocks, refs = refs[: len(lefts) + len(rights)], refs[len(lefts) + len(rights) :]
     outs, refs = refs[:-SCRATCH], refs[-SCRATCH:]
     row_out, col_out = refs[-2:] if last else outs
-    (lbuf, rbuf, sc, row_t, col_t, chk, row_f, row_m, row_s, col_f, col_m, col_s, waited, lsem, rsem) = refs[:-2]
+    (lbuf, rbuf, sc, row_t, col_t, chk, row_f, row_m, row_s, col_f, col_m, col_s, waited, shifted, lsem, rsem) = refs[:-2]
 
     def copies(side, slot):
         pieces = lefts if side == 0 else rights
@@ -208,7 +182,8 @@
 
         def sums(i):
             cols = jnp.zeros((8, width), jnp.float32)
-            size = jnp.zeros((8, 128), jnp.float32)
+            most = jnp.zeros((8, 128), jnp.float32)
+            least = jnp.full((8, 128), MOST, jnp.float32)
             for g in range(CH // G):
                 at = i * CH + g * G
                 v = sc[at : at + G, :width]
@@ -216,19 +191,24 @@
                     r_at = lax.broadcasted_iota(jnp.int32, (G, width), 0) + at
                     c_at = lax.broadcasted_iota(jnp.int32, (G, width), 1)
                     eye = r_at == c_at
-                    absv = jnp.where(eye, 0.0, jnp.abs(v))
                     v = jnp.where(eye, MASKED, v)
                     sc[at : at + G, :width] = v
-                else:
-                    absv = jnp.abs(v)
                 e = jnp.exp2(v * GAIN)
-                row_t[at : at + G, :] = lanes(e, jnp.add)
+                part = lanes(e, jnp.add)
+                row_t[at : at + G, :] = part
                 if not diag:
                     cols = cols + rows8(e, jnp.add)
-                size = jnp.maximum(size, rows8(lanes(absv, jnp.maximum), jnp.maximum))
+                most = jnp.maximum(most, rows8(part, jnp.maximum))
+                least = jnp.minimum(least, rows8(part, jnp.minimum))
             if not diag:
-                col_t[:, :width] = cols if i == 0 else col_t[:, :width] + cols
-            chk[...] = size if i == 0 else jnp.maximum(chk[...], size)
+                if i:
+                    cols = col_t[:, :width] + cols
+                col_t[:, :width] = cols
+                if i == B // CH - 1:
+                    least = jnp.minimum(least, lanes(cols, jnp.minimum))
+            if i:
+                most, least = jnp.maximum(chk[0], most), jnp.minimum(chk[1], least)
+            chk[0], chk[1] = most, least
 
         n = B // CH
         dot(0)
@@ -236,7 +216,8 @@
             if i + 1 < n:
                 dot(i + 1)
             sums(i)
-        plain = jnp.max(chk[...]) <= PLAIN
+        safe = jnp.logical_and(chk[0] <= MOST, chk[1] >= LEAST)
+        plain = jnp.max(jnp.where(safe, 0.0, 1.0)) == 0.0
 
         @pl.when(plain)
         def _():
@@ -246,6 +227,12 @@
 
         @pl.when(jnp.logical_not(plain))
         def _():
+            @pl.when(shifted[0] == 0)
+            def _():
+                row_s[...] = jnp.zeros_like(row_s)
+                row_m[...] = jnp.full_like(row_m, FLOOR)
+                shifted[0] = 1
+
             def group(g, _):
                 at = pl.multiple_of(g * G, G)
                 w = sc[pl.ds(at, G), :width] * GAIN
@@ -294,8 +281,7 @@
         @pl.when(needed)
         def _():
             row_f[...] = jnp.zeros_like(row_f)
-            row_s[...] = jnp.zeros_like(row_s)
-            row_m[...] = jnp.full_like(row_m, FLOOR)
+            shifted[0] = 0
             for s in range(nl):
 
                 @pl.when(q == s)
@@ -325,7 +311,14 @@
                     return 0
 
                 lax.fori_loop(start, stop, step, 0)
-            row_out[pl.ds(q, 1), :] = fold(row_m[...].T, row_s[...].T, row_f[...].T, 0)
+
+            @pl.when(shifted[0] == 0)
+            def _():
+                row_out[pl.ds(q, 1), :] = jnp.log2(jnp.sum(row_f[...].T, 0, keepdims=True))
+
+            @pl.when(shifted[0] > 0)
+            def _():
+                row_out[pl.ds(q, 1), :] = fold(row_m[...].T, row_s[...].T, row_f[...].T, 0)
 
         return 0
 
@@ -369,6 +362,7 @@
     widths = tuple(sum(piece[3] for piece in pieces) for pieces in rights)
     nrow, ncol = tuple(p.shape[0] for p in row_prev), tuple(p.shape[0] for p in col_prev)
     plan = (nl, nr, tables[0], tables[1], widths, nrow, ncol, own_first, last)
+    cost = 2 * B * B * D * 4 if own_first else B
     f32 = jnp.float32
     shapes = [(RING, 1, B), (1, B), (1, B)] if last else [(nl, B), (nr, B)]
     shapes = [jax.ShapeDtypeStruct(shape, f32) for shape in shapes]
@@ -385,7 +379,7 @@
             pltpu.VMEM((B, B), f32),
             pltpu.VMEM((B, 128), f32),
             pltpu.VMEM((8, B), f32),
-            pltpu.VMEM((8, 128), f32),
+            pltpu.VMEM((2, 8, 128), f32),
             pltpu.VMEM((B, 128), f32),
             pltpu.VMEM((B, 128), f32),
             pltpu.VMEM((B, 128), f32),
@@ -393,6 +387,7 @@
             pltpu.VMEM((nr, 8, B), f32),
             pltpu.VMEM((nr, 8, B), f32),
             pltpu.SMEM((nr,), jnp.int32),
+            pltpu.SMEM((1,), jnp.int32),
             pltpu.SemaphoreType.DMA((nl,)),
             pltpu.SemaphoreType.DMA((nr,)),
             pltpu.VMEM((nl, B), f32),
@@ -400,7 +395,7 @@
         ],
         compiler_params=pltpu.CompilerParams(vmem_limit_bytes=GRANT),
         cost_estimate=pl.CostEstimate(
-            flops=2 * B * B * D * max(1, nl * nr // 4), bytes_accessed=2 * B * D * (nl + nr), transcendentals=0
+            flops=cost, bytes_accessed=B, transcendentals=0
         ),
         name=name,
     )(live, *row_prev, *col_prev, *flat)
@@ -423,18 +418,14 @@
     me = lax.axis_index("dp")
     column = me % RING
     swap = along(0, 1)
-
-    a = send(unit, around(1))
-    b = send(unit, around(-1))
-    c = send(unit, along(-RING))
+    together = lax.optimization_barrier
+
     over, on = [], []
     for d in range(2 * RING, COUNT):
         z, y = d // 32, (d // RING) % 4
         relay = (z - (y < 2)) * 32 + (y + 1) % 4 * RING + d % RING
         over.append((d, relay))
         on.append((relay, d - 2 * RING))
-    relayed = send(low, over)
-    sib = send(unit, swap)
 
     targets = me + RING * jnp.array([0, 1, 2, 2], jnp.int32)
 
@@ -445,42 +436,54 @@
     def whole(array):
         return [(array, 0, 0, B)]
 
-    rights = [whole(unit)]
-    row_0, _ = stage("own", jnp.ones((1,), jnp.int32), rights, rights, own_first=True)
-    relayed, sib, row_0 = lax.optimization_barrier((relayed, sib, row_0))
+    def joined(upper, lower):
+        return [(upper, 0, 0, H), (lower, 0, H, H)]
+
+    a_top = send(top, around(1))
+    b_low = send(low, around(-1))
+    c_top = send(top, along(-RING))
+    relayed = send(low, over)
+    sib = send(unit, swap)
+    first_pairs = pairs_of(unit, sib)
+    lefts = [whole(unit), whole(sib)]
+    row_0, col_0 = stage("own", first_pairs[:, 0], lefts, [whole(unit)], own_first=True)
+
+    a_top, b_low, c_top, relayed, row_0 = together((a_top, b_low, c_top, relayed, row_0))
+    top, low, _ = together((top, low, c_top))
+    a_low = send(low, around(1))
+    b_top = send(top, around(-1))
+    c_low = send(low, along(-RING))
     d_low = send(relayed, on)
-    sib_pairs = pairs_of(sib)
-    row_1, col_1 = stage("sibling", sib_pairs[0, :1], [whole(sib)], rights)
-    a, b, c, d_low, row_1 = lax.optimization_barrier((a, b, c, d_low, row_1))
-
-    a_top, b_low = halves(a, b)
+    a_top_sib = send(a_top, swap)
+
+    a_low, a_top_sib = together((a_low, a_top_sib))
+    a_top, b_low, a_low = together((a_top, b_low, a_low))
     f_top = send(a_top, around(1))
+    a_low_sib = send(a_low, swap)
+    b_low_sib = send(b_low, swap)
+    b_low, b_top, a_low = together((b_low, b_top, a_low))
     f_low = send(b_low, around(-1))
-    top, a, b, a_top = lax.optimization_barrier((top, a, b, a_top))
+    b_top_sib = send(b_top, swap)
+    c_low, d_low, a_low, b_top = together((c_low, d_low, a_low, b_top))
+    top, _ = together((top, c_low))
     d_top = send(top, along(-2 * RING))
-    a_sib = send(a, swap)
-    b_sib = send(b, swap)
-
-    rights = rights + [whole(c), [(d_low, 0, 0, H)]]
-    early = jnp.concatenate([pairs_of(unit), sib_pairs, pairs_of(a, b)], 0)
-    live = early.at[:2, :1].set(0)[:, :3]
-    lefts = [whole(unit), whole(sib), whole(a), whole(b)]
-    row_2, col_2 = stage("near", live.reshape(-1), lefts, rights, [row_0, row_1], [col_1])
-    a_sib, b_sib, row_2 = lax.optimization_barrier((a_sib, b_sib, row_2))
-    more = pairs_of(a_sib, b_sib)
-    row_3, col_3 = stage("mid", more[:, :3].reshape(-1), [whole(a_sib), whole(b_sib)], rights, [], [col_2])
-    f_top, f_low, d_top, row_3 = lax.optimization_barrier((f_top, f_low, d_top, row_3))
+
+    rights = [whole(unit), joined(c_top, c_low), [(d_low, 0, 0, H)]]
+    lefts += [joined(a_top, a_low), joined(b_top, b_low)]
+    lefts += [joined(a_top_sib, a_low_sib), joined(b_top_sib, b_low_sib)]
+    near_pairs = jnp.concatenate([first_pairs, pairs_of(a_low, b_low, a_low_sib, b_low_sib)], 0)
+    live = near_pairs.at[:2, :1].set(0)[:, :3]
+    row_2, col_2 = stage("near", live.reshape(-1), lefts, rights, [row_0], [col_0])
+    f_top, f_low, d_top, row_2 = together((f_top, f_low, d_top, row_2))
     f_top_sib = send(f_top, swap)
     f_low_sib = send(f_low, swap)
 
     rights = rights + [[(d_top, 0, 0, H)]]
-    lefts = lefts + [whole(a_sib), whole(b_sib)]
-    lefts = lefts + [[(f_top, 0, 0, H), (f_low, 0, H, H)], [(f_top_sib, 0, 0, H), (f_low_sib, 0, H, H)]]
-    early = jnp.concatenate([early, more], 0).at[:, :3].set(0)
-    live = jnp.concatenate([early, pairs_of(f_low, f_low_sib)], 0)
+    lefts = lefts + [joined(f_top, f_low), joined(f_top_sib, f_low_sib)]
+    live = jnp.concatenate([near_pairs.at[:, :3].set(0), pairs_of(f_low, f_low_sib)], 0)
     place = jnp.stack([column // 2, column % 2]).astype(jnp.int32)
     live = jnp.concatenate([live.reshape(-1), place])
-    ring_part, next_part, after_part = stage("far", live, lefts, rights, [row_2, row_3], [col_3], last=True)
+    ring_part, next_part, after_part = stage("far", live, lefts, rights, [row_2], [col_2], last=True)
 
     next_got = send(next_part, along(RING))
     after_got = send(after_part, along(2 * RING))

time: 144 us -> 144 us (level)
  Pallas kernels: 43.6 us -> 48.9 us
  starting transfers between devices: 37.3 us -> 32.3 us
  other arithmetic: 3.35 us -> 1.34 us
    pallas_call x5 -> x3, Pallas kernels: 35.2 us -> 43.5 us  [stage(): pl.pallas_call(functools.partial(stage_kernel, plan), out_shape=shapes, i...]
    all_to_all x1, starting transfers between devices: 10.2 us -> 3.31 us  [body(): lax.all_to_all(ring_part, 'dp', 0, 0, axis_index_groups=groups, tiled=True)]
    pallas_call x1 -> x0, Pallas kernels: 2.79 us -> none  [halves(): pl.pallas_call(halves_kernel, in_specs=[anywhere] * 2, out_specs=[anywher...]
    unnamed x18 -> x25, local copies, waits for them, and re-layouts: 2.58 us -> 4.91 us
    ppermute x15 -> x20, starting transfers between devices: 27.2 us -> 29 us  [send(): return lax.ppermute(value, 'dp', moves)]
    slice x6 -> x8, local copies, waits for them, and re-layouts: 3.35 us -> 1.98 us  [pairs_of(): x[-LIST:1 - LIST, :16]]
    ppermute x15 -> x20, waiting for transfers between devices: 50.4 us -> 51.4 us  [send(): return lax.ppermute(value, 'dp', moves)]
  transfers between devices with their start and end apart: 16 -> 21, of which waited for: 9 -> 11; matrix products, arithmetic and copies ran while one was open for 6% -> 3% of each run, Pallas kernels for 16% -> 17%
where the time goes in v1:
time: 144 us
  waiting for transfers between devices  51.4 us (36%)
  Pallas kernels  48.9 us (34%)
  starting transfers between devices  32.3 us (22%)
  local copies, waits for them, and re-layouts  8.58 us (6%)
    ppermute x20, waiting for transfers between devices, send(): return lax.ppermute(value, 'dp', moves)  51.4 us
    pallas_call x3, Pallas kernels, stage(): pl.pallas_call(functools.partial(stage_kernel, plan), out_shape=shapes, i...  43.5 us
    ppermute x20, starting transfers between devices, send(): return lax.ppermute(value, 'dp', moves)  29 us
    unnamed x25, local copies, waits for them, and re-layouts  4.91 us
    pallas_call x1, Pallas kernels, normalize(): pl.pallas_call(unit_kernel, in_specs=[smem, smem, anywhere], out_specs=[a...  4.02 us
    all_to_all x1, starting transfers between devices, body(): lax.all_to_all(ring_part, 'dp', 0, 0, axis_index_groups=groups, tiled=True)  3.31 us
  transfers between devices with their start and end apart: 21, of which 11 were waited for; matrix products, arithmetic and copies ran while one was open for 3% of the time, Pallas kernels for 17%

profile of v1, /device:TPU:34, one launch (start us, length us, event | category | flops | bytes accessed | tf_op | source)
XLA Modules:
  0.0 143.5 jit_solution(8685834714409169002)
XLA Ops:
  0.7 4.0 %unit_rows.1 = (bf16[1040,1024]{1,0:T(8,128)(2,1)}, bf16[512,1024]{1,0:T(8,128)(2,1)}, bf16[528,1024]{1,0:T(8,128)(2,1)}) custom-call(s32[1,13]{1,0:T(1,128)} %list_ref.1, s32[1]{0:T(128)S(6)} %copy.7.count_ref, bf16[1024,1024]{1,0:T(8,128)(2,1)} %x_ref.1), custom_call_target="tpu_custom_call" | custom-call | tf_op jit(solution)/shard_map/unit_rows/pallas_call | solution.py:86
  4.7 0.1 collective-permute-start
  4.8 4.5 %collective-permute-start.3 = (bf16[512,1024]{1,0:T(8,128)(2,1)}, bf16[512,1024]{1,0:T(8,128)(2,1)}, u32[]{:S(2)}, u32[]{:S(2)}) collective-permute-start(bf16[512,1024]{1,0:T(8,128)(2,1)} %get-tuple-element.82), channel_id=1, source_target_pairs={{8,0},{9,1},{10,2},{11,3},{12,4},{13,5},{14,6},{15,7},{16,8},{17,9... | collective-permute-start | bytes 3145736 | tf_op jit(solution)/shard_map/ppermute | solution.py:45
  9.3 1.6 %collective-permute-start.1 = (bf16[512,1024]{1,0:T(8,128)(2,1)}, bf16[512,1024]{1,0:T(8,128)(2,1)}, u32[]{:S(2)}, u32[]{:S(2)}) collective-permute-start(bf16[512,1024]{1,0:T(8,128)(2,1)} %get-tuple-element.82), channel_id=1, source_target_pairs={{0,2},{1,3},{2,4},{3,5},{4,6},{5,7},{6,0},{7,1},{8,10},{9,11},{10,... | collective-permute-start | bytes 3145736 | tf_op jit(solution)/shard_map/ppermute | solution.py:45
  10.8 1.9 %collective-permute-start.4 = (bf16[528,1024]{1,0:T(8,128)(2,1)}, bf16[528,1024]{1,0:T(8,128)(2,1)}, u32[]{:S(2)}, u32[]{:S(2)}) collective-permute-start(bf16[528,1024]{1,0:T(8,128)(2,1)} %get-tuple-element.68), channel_id=1, source_target_pairs={{16,24},{17,25},{18,26},{19,27},{20,28},{21,29},{22,30},{23,31},{2... | collective-permute-start | bytes 3244040 | tf_op jit(solution)/shard_map/ppermute | solution.py:45
  12.7 0.6 collective-permute-start.2
  13.3 0.6 slice.69
  14.0 0.0 collective-permute-done.refs_1_.refs_3_
  14.0 1.3 copy-done
  15.3 0.2 compare_reduce_fusion.2
  15.5 0.7 slice_reduce_fusion.live
  16.2 8.0 %own.1 = (f32[2,1024]{1,0:T(2,128)}, f32[1,1024]{1,0:T(1,128)}) custom-call(s32[2]{0:T(128)} %slice_reduce_fusion.live, bf16[1040,1024]{1,0:T(8,128)(2,1)} %get-tuple-element.63.refs_0_.refs_2_.refs_12_.refs_16_, bf16[1040,1024]{1,0:T(8,128)(2,1)} %copy-done, bf16[1040,1024]{1,0:T(8,128)(2,1)} %get-tuple-element.63.refs_0_.refs_2_.refs_12_.refs_16_), custom_call_target="tpu_custom_call" | custom-call | flops 8589934592 | bytes 1024 | tf_op jit(solution)/shard_map/own/pallas_call | solution.py:369
  24.2 8.4 %collective-permute-done.3.refs_13_.refs_17_ = bf16[512,1024]{1,0:T(8,128)(2,1)} collective-permute-done((bf16[512,1024]{1,0:T(8,128)(2,1)}, bf16[512,1024]{1,0:T(8,128)(2,1)}, u32[]{:S(2)}, u32[]{:S(2)}) %collective-permute-start.3) | collective-permute-done | bytes 1048608 | tf_op jit(solution)/shard_map/ppermute | solution.py:45
  32.6 2.3 %collective-permute-done.1.refs_4_ = bf16[512,1024]{1,0:T(8,128)(2,1)} collective-permute-done((bf16[512,1024]{1,0:T(8,128)(2,1)}, bf16[512,1024]{1,0:T(8,128)(2,1)}, u32[]{:S(2)}, u32[]{:S(2)}) %collective-permute-start.1) | collective-permute-done | bytes 1048608 | tf_op jit(solution)/shard_map/ppermute | solution.py:45
  34.9 5.0 %collective-permute-done.4 = bf16[528,1024]{1,0:T(8,128)(2,1)} collective-permute-done((bf16[528,1024]{1,0:T(8,128)(2,1)}, bf16[528,1024]{1,0:T(8,128)(2,1)}, u32[]{:S(2)}, u32[]{:S(2)}) %collective-permute-start.4) | collective-permute-done | bytes 1081376 | tf_op jit(solution)/shard_map/ppermute | solution.py:45
  39.9 0.0 collective-permute-done.2.refs_7_
  39.9 1.2 collective-permute-start.7
  41.1 0.0 collective-permute-start.8
  41.1 1.9 %collective-permute-start.5 = (bf16[528,1024]{1,0:T(8,128)(2,1)}, bf16[528,1024]{1,0:T(8,128)(2,1)}, u32[]{:S(2)}, u32[]{:S(2)}) collective-permute-start(bf16[528,1024]{1,0:T(8,128)(2,1)} %get-tuple-element.68), channel_id=1, source_target_pairs={{8,0},{9,1},{10,2},{11,3},{12,4},{13,5},{14,6},{15,7},{16,8},{17,9... | collective-permute-start | bytes 3244040 | tf_op jit(solution)/shard_map/ppermute | solution.py:45
  43.1 0.9 collective-permute-start.9
  43.9 3.9 %collective-permute-start.6 = (bf16[528,1024]{1,0:T(8,128)(2,1)}, bf16[528,1024]{1,0:T(8,128)(2,1)}, u32[]{:S(2)}, u32[]{:S(2)}) collective-permute-start(bf16[528,1024]{1,0:T(8,128)(2,1)} %collective-permute-done.4), channel_id=1, source_target_pairs={{24,0},{25,1},{26,2},{27,3},{28,4},{29,5},{30,6},{31,7},{0,8},{1,9... | collective-permute-start | bytes 3244040 | tf_op jit(solution)/shard_map/ppermute | solution.py:45
  47.9 0.0 collective-permute-done.8.refs_8_
  47.9 17.1 %collective-permute-done.7.refs_5_ = bf16[528,1024]{1,0:T(8,128)(2,1)S(1)} collective-permute-done((bf16[528,1024]{1,0:T(8,128)(2,1)}, bf16[528,1024]{1,0:T(8,128)(2,1)S(1)}, u32[]{:S(2)}, u32[]{:S(2)}) %collective-permute-start.7) | collective-permute-done | bytes 1081376 | tf_op jit(solution)/shard_map/ppermute | solution.py:45
  65.0 0.0 collective-permute-start.11
  65.0 0.5 collective-permute-start.10
  65.5 3.4 %collective-permute-done.9.refs_6_ = bf16[512,1024]{1,0:T(8,128)(2,1)S(1)} collective-permute-done((bf16[512,1024]{1,0:T(8,128)(2,1)}, bf16[512,1024]{1,0:T(8,128)(2,1)S(1)}, u32[]{:S(2)}, u32[]{:S(2)}) %collective-permute-start.9) | collective-permute-done | bytes 1048608 | tf_op jit(solution)/shard_map/ppermute | solution.py:45
  68.9 0.8 collective-permute-start.13
  69.7 0.0 collective-permute-done.5.refs_14_.refs_18_
  69.7 0.0 collective-permute-start.15
  69.7 3.6 %collective-permute-done.6.refs_15_.refs_19_ = bf16[528,1024]{1,0:T(8,128)(2,1)} collective-permute-done((bf16[528,1024]{1,0:T(8,128)(2,1)}, bf16[528,1024]{1,0:T(8,128)(2,1)}, u32[]{:S(2)}, u32[]{:S(2)}) %collective-permute-start.6) | collective-permute-done | bytes 1081376 | tf_op jit(solution)/shard_map/ppermute | solution.py:45
  73.4 1.2 collective-permute-start.12
  74.5 0.0 collective-permute-done.11.refs_11_
  74.6 2.6 %collective-permute-start.14 = (bf16[512,1024]{1,0:T(8,128)(2,1)}, bf16[512,1024]{1,0:T(8,128)(2,1)}, u32[]{:S(2)}, u32[]{:S(2)}) collective-permute-start(bf16[512,1024]{1,0:T(8,128)(2,1)} %get-tuple-element.82), channel_id=1, source_target_pairs={{16,0},{17,1},{18,2},{19,3},{20,4},{21,5},{22,6},{23,7},{24,8},{25... | collective-permute-start | bytes 3145736 | tf_op jit(solution)/shard_map/ppermute | solution.py:45
  77.2 0.7 slice.73
  77.9 0.0 collective-permute-done.10.refs_9_
  77.9 1.0 copy-done.3
  78.9 0.2 compare_reduce_fusion
  79.2 0.2 scatter.9
  79.3 0.7 reshape.120.live
  80.0 0.0 collective-permute-done.15.refs_10_
  80.0 1.0 copy-done.6
  81.0 16.3 %near.1 = (f32[6,1024]{1,0:T(8,128)}, f32[3,1024]{1,0:T(4,128)}) custom-call(s32[18]{0:T(128)} %reshape.120.live, f32[2,1024]{1,0:T(2,128)} %get-tuple-element.83.refs_0_, f32[1,1024]{1,0:T(1,128)} %get-tuple-element.84.refs_1_, bf16[1040,1024]{1,0:T(8,128)(2,1)} %get-tuple-element.63.refs_0_.refs_2_.refs_12_.refs_16_, bf16[1040,1024]{1,0:T(8,128)(2,1)} %copy-done, ...), custom_call_target="tpu_custom_call" | custom-call | flops 1024 | bytes 1024 | tf_op jit(solution)/shard_map/near/pallas_call | solution.py:369
  97.2 0.9 collective-permute-done.12.refs_12_
  98.1 4.3 %collective-permute-done.14.refs_20_ = bf16[512,1024]{1,0:T(8,128)(2,1)} collective-permute-done((bf16[512,1024]{1,0:T(8,128)(2,1)}, bf16[512,1024]{1,0:T(8,128)(2,1)}, u32[]{:S(2)}, u32[]{:S(2)}) %collective-permute-start.14) | collective-permute-done | bytes 1048608 | tf_op jit(solution)/shard_map/ppermute | solution.py:45
  102.5 0.0 collective-permute-done.13.refs_13_
  102.5 0.0 collective-permute-start.16
  102.5 0.5 collective-permute-start.17
  103.0 0.7 slice.77
  103.6 0.1 scatter.6
  103.7 3.1 %collective-permute-done.16.refs_15_ = bf16[528,1024]{1,0:T(8,128)(2,1)S(1)} collective-permute-done((bf16[528,1024]{1,0:T(8,128)(2,1)}, bf16[528,1024]{1,0:T(8,128)(2,1)S(1)}, u32[]{:S(2)}, u32[]{:S(2)}) %collective-permute-start.16) | collective-permute-done | bytes 1081376 | tf_op jit(solution)/shard_map/ppermute | solution.py:45
  106.9 1.0 copy-done.7
  107.9 0.2 compare_reduce_fusion.1
  108.1 0.1 reshape.121
  108.2 0.7 pad_add_fusion.2.live
  108.9 19.2 %far.1 = (f32[8,1,1024]{2,1,0:T(1,128)}, f32[1,1024]{1,0:T(1,128)}, f32[1,1024]{1,0:T(1,128)}) custom-call(s32[34]{0:T(128)} %pad_add_fusion.2.live, f32[6,1024]{1,0:T(8,128)} %get-tuple-element.90.refs_0_, f32[3,1024]{1,0:T(4,128)} %get-tuple-element.91.refs_1_, bf16[1040,1024]{1,0:T(8,128)(2,1)} %get-tuple-element.63.refs_0_.refs_2_.refs_12_.refs_16_, ...), custom_call_target="tpu_custom_call" | custom-call | flops 1024 | bytes 1024 | tf_op jit(solution)/shard_map/far/pallas_call | solution.py:369
  128.1 3.3 %all-to-all-start = ((f32[8,1,1024]{2,1,0:T(1,128)}), f32[8,1,1024]{2,1,0:T(1,128)S(1)}, u32[]{:S(2)}, u32[]{:S(2)}) async-start(f32[8,1,1024]{2,1,0:T(1,128)} %get-tuple-element.94), calls=%async_computation | async-start | bytes 65536 | tf_op jit(solution)/shard_map/all_to_all | solution.py:491
  131.4 1.9 %collective-permute-start.18 = (f32[1,1024]{1,0:T(1,128)}, f32[1,1024]{1,0:T(1,128)S(1)}, u32[]{:S(2)}, u32[]{:S(2)}) collective-permute-start(f32[1,1024]{1,0:T(1,128)} %get-tuple-element.95), channel_id=1, source_target_pairs={{0,8},{1,9},{2,10},{3,11},{4,12},{5,13},{6,14},{7,15},{8,16},{9,17... | collective-permute-start | bytes 12296 | tf_op jit(solution)/shard_map/ppermute | solution.py:45
  133.4 4.9 %collective-permute-start.19 = (f32[1,1024]{1,0:T(1,128)}, f32[1,1024]{1,0:T(1,128)S(1)}, u32[]{:S(2)}, u32[]{:S(2)}) collective-permute-start(f32[1,1024]{1,0:T(1,128)} %get-tuple-element.96), channel_id=1, source_target_pairs={{0,16},{1,17},{2,18},{3,19},{4,20},{5,21},{6,22},{7,23},{8,24},{9,... | collective-permute-start | bytes 12296 | tf_op jit(solution)/shard_map/ppermute | solution.py:45
  138.2 1.0 collective-permute-done.18.refs_0_
  139.2 2.2 %collective-permute-done.19.refs_1_ = f32[1,1024]{1,0:T(1,128)S(1)} collective-permute-done((f32[1,1024]{1,0:T(1,128)}, f32[1,1024]{1,0:T(1,128)S(1)}, u32[]{:S(2)}, u32[]{:S(2)}) %collective-permute-start.19) | collective-permute-done | bytes 4128 | tf_op jit(solution)/shard_map/ppermute | solution.py:45
  141.5 0.0 all-to-all-done.ring_ref
  141.5 0.6 copy-done.10
  142.1 0.0 copy-done.8
  142.1 1.4 last_sum.1
  (36 shorter events, 0.1 us)
Async XLA Ops:
  0.0 14.0 %copy-start.11 = (s32[4]{0:T(128)S(1)}, s32[4]{0:T(128)}, u32[]{:S(2)}) copy-start(s32[4]{0:T(128)} %constant.109) | copy-start | bytes 52
  4.7 9.3 %collective-permute-start = (bf16[1040,1024]{1,0:T(8,128)(2,1)}, bf16[1040,1024]{1,0:T(8,128)(2,1)S(1)}, u32[]{:S(2)}, u32[]{:S(2)}) collective-permute-start(bf16[1040,1024]{1,0:T(8,128)(2,1)} %get-tuple-element.63.refs_0_.refs_2_.refs_12_.refs_16_), channel_id=1, source_target_pairs={{0,1},{1,0},{2,3},{3,2},{4,5},{5,4},{6,7},{7,6},{8,9},{9,8},{10,11... | collective-permute-start | bytes 6389768 | tf_op jit(solution)/shard_map/ppermute | solution.py:45
  4.8 27.8 %collective-permute-start.3 = (bf16[512,1024]{1,0:T(8,128)(2,1)}, bf16[512,1024]{1,0:T(8,128)(2,1)}, u32[]{:S(2)}, u32[]{:S(2)}) collective-permute-start(bf16[512,1024]{1,0:T(8,128)(2,1)} %get-tuple-element.82), channel_id=1, source_target_pairs={{8,0},{9,1},{10,2},{11,3},{12,4},{13,5},{14,6},{15,7},{16,8},{17,9... | collective-permute-start | bytes 3145736 | tf_op jit(solution)/shard_map/ppermute | solution.py:45
  9.3 25.7 %collective-permute-start.1 = (bf16[512,1024]{1,0:T(8,128)(2,1)}, bf16[512,1024]{1,0:T(8,128)(2,1)}, u32[]{:S(2)}, u32[]{:S(2)}) collective-permute-start(bf16[512,1024]{1,0:T(8,128)(2,1)} %get-tuple-element.82), channel_id=1, source_target_pairs={{0,2},{1,3},{2,4},{3,5},{4,6},{5,7},{6,0},{7,1},{8,10},{9,11},{10,... | collective-permute-start | bytes 3145736 | tf_op jit(solution)/shard_map/ppermute | solution.py:45
  10.8 29.1 %collective-permute-start.4 = (bf16[528,1024]{1,0:T(8,128)(2,1)}, bf16[528,1024]{1,0:T(8,128)(2,1)}, u32[]{:S(2)}, u32[]{:S(2)}) collective-permute-start(bf16[528,1024]{1,0:T(8,128)(2,1)} %get-tuple-element.68), channel_id=1, source_target_pairs={{16,24},{17,25},{18,26},{19,27},{20,28},{21,29},{22,30},{23,31},{2... | collective-permute-start | bytes 3244040 | tf_op jit(solution)/shard_map/ppermute | solution.py:45
  12.7 27.2 %collective-permute-start.2 = (bf16[528,1024]{1,0:T(8,128)(2,1)}, bf16[528,1024]{1,0:T(8,128)(2,1)}, u32[]{:S(2)}, u32[]{:S(2)}) collective-permute-start(bf16[528,1024]{1,0:T(8,128)(2,1)} %get-tuple-element.68), channel_id=1, source_target_pairs={{0,6},{1,7},{2,0},{3,1},{4,2},{5,3},{6,4},{7,5},{8,14},{9,15},{10,... | collective-permute-start | bytes 3244040 | tf_op jit(solution)/shard_map/ppermute | solution.py:45
  14.0 1.3 copy-start
  39.9 25.0 %collective-permute-start.7 = (bf16[528,1024]{1,0:T(8,128)(2,1)}, bf16[528,1024]{1,0:T(8,128)(2,1)S(1)}, u32[]{:S(2)}, u32[]{:S(2)}) collective-permute-start(bf16[528,1024]{1,0:T(8,128)(2,1)} %get-tuple-element.68), channel_id=1, source_target_pairs={{0,2},{1,3},{2,4},{3,5},{4,6},{5,7},{6,0},{7,1},{8,10},{9,11},{10,... | collective-permute-start | bytes 3244040 | tf_op jit(solution)/shard_map/ppermute | solution.py:45
  41.1 6.7 %collective-permute-start.8 = (bf16[512,1024]{1,0:T(8,128)(2,1)}, bf16[512,1024]{1,0:T(8,128)(2,1)S(1)}, u32[]{:S(2)}, u32[]{:S(2)}) collective-permute-start(bf16[512,1024]{1,0:T(8,128)(2,1)} %collective-permute-done.1.refs_4_), channel_id=1, source_target_pairs={{0,1},{1,0},{2,3},{3,2},{4,5},{5,4},{6,7},{7,6},{8,9},{9,8},{10,11... | collective-permute-start | bytes 3145736 | tf_op jit(solution)/shard_map/ppermute | solution.py:45
  41.1 28.6 %collective-permute-start.5 = (bf16[528,1024]{1,0:T(8,128)(2,1)}, bf16[528,1024]{1,0:T(8,128)(2,1)}, u32[]{:S(2)}, u32[]{:S(2)}) collective-permute-start(bf16[528,1024]{1,0:T(8,128)(2,1)} %get-tuple-element.68), channel_id=1, source_target_pairs={{8,0},{9,1},{10,2},{11,3},{12,4},{13,5},{14,6},{15,7},{16,8},{17,9... | collective-permute-start | bytes 3244040 | tf_op jit(solution)/shard_map/ppermute | solution.py:45
  43.1 25.9 %collective-permute-start.9 = (bf16[512,1024]{1,0:T(8,128)(2,1)}, bf16[512,1024]{1,0:T(8,128)(2,1)S(1)}, u32[]{:S(2)}, u32[]{:S(2)}) collective-permute-start(bf16[512,1024]{1,0:T(8,128)(2,1)} %get-tuple-element.82), channel_id=1, source_target_pairs={{0,6},{1,7},{2,0},{3,1},{4,2},{5,3},{6,4},{7,5},{8,14},{9,15},{10,... | collective-permute-start | bytes 3145736 | tf_op jit(solution)/shard_map/ppermute | solution.py:45
  43.9 29.4 %collective-permute-start.6 = (bf16[528,1024]{1,0:T(8,128)(2,1)}, bf16[528,1024]{1,0:T(8,128)(2,1)}, u32[]{:S(2)}, u32[]{:S(2)}) collective-permute-start(bf16[528,1024]{1,0:T(8,128)(2,1)} %collective-permute-done.4), channel_id=1, source_target_pairs={{24,0},{25,1},{26,2},{27,3},{28,4},{29,5},{30,6},{31,7},{0,8},{1,9... | collective-permute-start | bytes 3244040 | tf_op jit(solution)/shard_map/ppermute | solution.py:45
  47.9 26.7 %copy-start.4 = (bf16[512,1024]{1,0:T(8,128)(2,1)}, bf16[512,1024]{1,0:T(8,128)(2,1)S(1)}, u32[]{:S(2)}) copy-start(bf16[512,1024]{1,0:T(8,128)(2,1)S(1)} %collective-permute-done.8.refs_8_) | copy-start | bytes 3145732
  65.0 12.9 %copy-start.1 = (bf16[528,1024]{1,0:T(8,128)(2,1)}, bf16[528,1024]{1,0:T(8,128)(2,1)S(1)}, u32[]{:S(2)}) copy-start(bf16[528,1024]{1,0:T(8,128)(2,1)S(1)} %collective-permute-done.7.refs_5_) | copy-start | bytes 3244036
  65.0 9.6 %collective-permute-start.11 = (bf16[528,1024]{1,0:T(8,128)(2,1)}, bf16[528,1024]{1,0:T(8,128)(2,1)S(1)}, u32[]{:S(2)}, u32[]{:S(2)}) collective-permute-start(bf16[528,1024]{1,0:T(8,128)(2,1)} %collective-permute-done.2.refs_7_), channel_id=1, source_target_pairs={{0,1},{1,0},{2,3},{3,2},{4,5},{5,4},{6,7},{7,6},{8,9},{9,8},{10,11... | collective-permute-start | bytes 3244040 | tf_op jit(solution)/shard_map/ppermute | solution.py:45
  65.0 12.9 %collective-permute-start.10 = (bf16[528,1024]{1,0:T(8,128)(2,1)S(1)}, bf16[528,1024]{1,0:T(8,128)(2,1)S(1)}, u32[]{:S(2)}, u32[]{:S(2)}) collective-permute-start(bf16[528,1024]{1,0:T(8,128)(2,1)S(1)} %collective-permute-done.7.refs_5_), channel_id=1, source_target_pairs={{0,1},{1,0},{2,3},{3,2},{4,5},{5,4},{6,7},{7,6},{8,9},{9,8},{10,11... | collective-permute-start | bytes 3244040 | tf_op jit(solution)/shard_map/ppermute | solution.py:45
  68.9 10.0 %copy-start.5 = (bf16[512,1024]{1,0:T(8,128)(2,1)}, bf16[512,1024]{1,0:T(8,128)(2,1)S(1)}, u32[]{:S(2)}) copy-start(bf16[512,1024]{1,0:T(8,128)(2,1)S(1)} %collective-permute-done.9.refs_6_) | copy-start | bytes 3145732
  68.9 33.6 %collective-permute-start.13 = (bf16[528,1024]{1,0:T(8,128)(2,1)}, bf16[528,1024]{1,0:T(8,128)(2,1)}, u32[]{:S(2)}, u32[]{:S(2)}) collective-permute-start(bf16[528,1024]{1,0:T(8,128)(2,1)} %collective-permute-done.2.refs_7_), channel_id=1, source_target_pairs={{0,6},{1,7},{2,0},{3,1},{4,2},{5,3},{6,4},{7,5},{8,14},{9,15},{10,... | collective-permute-start | bytes 3244040 | tf_op jit(solution)/shard_map/ppermute | solution.py:45
  69.7 10.3 %collective-permute-start.15 = (bf16[512,1024]{1,0:T(8,128)(2,1)S(1)}, bf16[512,1024]{1,0:T(8,128)(2,1)S(1)}, u32[]{:S(2)}, u32[]{:S(2)}) collective-permute-start(bf16[512,1024]{1,0:T(8,128)(2,1)S(1)} %collective-permute-done.9.refs_6_), channel_id=1, source_target_pairs={{0,1},{1,0},{2,3},{3,2},{4,5},{5,4},{6,7},{7,6},{8,9},{9,8},{10,11... | collective-permute-start | bytes 3145736 | tf_op jit(solution)/shard_map/ppermute | solution.py:45
  73.4 24.8 %collective-permute-start.12 = (bf16[512,1024]{1,0:T(8,128)(2,1)}, bf16[512,1024]{1,0:T(8,128)(2,1)}, u32[]{:S(2)}, u32[]{:S(2)}) collective-permute-start(bf16[512,1024]{1,0:T(8,128)(2,1)} %collective-permute-done.1.refs_4_), channel_id=1, source_target_pairs={{0,2},{1,3},{2,4},{3,5},{4,6},{5,7},{6,0},{7,1},{8,10},{9,11},{10,... | collective-permute-start | bytes 3145736 | tf_op jit(solution)/shard_map/ppermute | solution.py:45
  74.6 3.3 %copy-start.2 = (bf16[528,1024]{1,0:T(8,128)(2,1)}, bf16[528,1024]{1,0:T(8,128)(2,1)S(1)}, u32[]{:S(2)}) copy-start(bf16[528,1024]{1,0:T(8,128)(2,1)S(1)} %collective-permute-done.11.refs_11_) | copy-start | bytes 3244036
  74.6 27.9 %collective-permute-start.14 = (bf16[512,1024]{1,0:T(8,128)(2,1)}, bf16[512,1024]{1,0:T(8,128)(2,1)}, u32[]{:S(2)}, u32[]{:S(2)}) collective-permute-start(bf16[512,1024]{1,0:T(8,128)(2,1)} %get-tuple-element.82), channel_id=1, source_target_pairs={{16,0},{17,1},{18,2},{19,3},{20,4},{21,5},{22,6},{23,7},{24,8},{25... | collective-permute-start | bytes 3145736 | tf_op jit(solution)/shard_map/ppermute | solution.py:45
  77.9 1.0 copy-start.3
  80.0 1.0 copy-start.6
  102.5 4.4 %collective-permute-start.16 = (bf16[528,1024]{1,0:T(8,128)(2,1)}, bf16[528,1024]{1,0:T(8,128)(2,1)S(1)}, u32[]{:S(2)}, u32[]{:S(2)}) collective-permute-start(bf16[528,1024]{1,0:T(8,128)(2,1)} %collective-permute-done.13.refs_13_), channel_id=1, source_target_pairs={{0,1},{1,0},{2,3},{3,2},{4,5},{5,4},{6,7},{7,6},{8,9},{9,8},{10,11... | collective-permute-start | bytes 3244040 | tf_op jit(solution)/shard_map/ppermute | solution.py:45
  102.5 6.4 %collective-permute-start.17 = (bf16[512,1024]{1,0:T(8,128)(2,1)}, bf16[512,1024]{1,0:T(8,128)(2,1)}, u32[]{:S(2)}, u32[]{:S(2)}) collective-permute-start(bf16[512,1024]{1,0:T(8,128)(2,1)} %collective-permute-done.12.refs_12_), channel_id=1, source_target_pairs={{0,1},{1,0},{2,3},{3,2},{4,5},{5,4},{6,7},{7,6},{8,9},{9,8},{10,11... | collective-permute-start | bytes 3145736 | tf_op jit(solution)/shard_map/ppermute | solution.py:45
  106.9 1.0 copy-start.7
  128.1 13.3 %all-to-all-start = ((f32[8,1,1024]{2,1,0:T(1,128)}), f32[8,1,1024]{2,1,0:T(1,128)S(1)}, u32[]{:S(2)}, u32[]{:S(2)}) async-start(f32[8,1,1024]{2,1,0:T(1,128)} %get-tuple-element.94), calls=%async_computation | async-start | bytes 65536 | tf_op jit(solution)/shard_map/all_to_all | solution.py:491
  131.4 7.8 %collective-permute-start.18 = (f32[1,1024]{1,0:T(1,128)}, f32[1,1024]{1,0:T(1,128)S(1)}, u32[]{:S(2)}, u32[]{:S(2)}) collective-permute-start(f32[1,1024]{1,0:T(1,128)} %get-tuple-element.95), channel_id=1, source_target_pairs={{0,8},{1,9},{2,10},{3,11},{4,12},{5,13},{6,14},{7,15},{8,16},{9,17... | collective-permute-start | bytes 12296 | tf_op jit(solution)/shard_map/ppermute | solution.py:45
  133.4 8.1 %collective-permute-start.19 = (f32[1,1024]{1,0:T(1,128)}, f32[1,1024]{1,0:T(1,128)S(1)}, u32[]{:S(2)}, u32[]{:S(2)}) collective-permute-start(f32[1,1024]{1,0:T(1,128)} %get-tuple-element.96), channel_id=1, source_target_pairs={{0,16},{1,17},{2,18},{3,19},{4,20},{5,21},{6,22},{7,23},{8,24},{9,... | collective-permute-start | bytes 12296 | tf_op jit(solution)/shard_map/ppermute | solution.py:45
  139.2 2.2 %copy-start.9 = (f32[1,1024]{1,0:T(1,128)}, f32[1,1024]{1,0:T(1,128)S(1)}, u32[]{:S(2)}) copy-start(f32[1,1024]{1,0:T(1,128)S(1)} %collective-permute-done.18.refs_0_) | copy-start | bytes 12292
  141.5 0.6 copy-start.10
  141.5 0.6 copy-start.8
